TPU v7x, 128 devices: a whole 4x4x4 slice. The times are simulated.
128 devices in a mesh: dp: 8 (over z, core), ctx: 16 (over y, x).
Axes of the slice: x: 4, y: 4, z: 4, core: 2. Of those that a mesh axis runs over, the one named last changes fastest.
Arguments:
- attn_in: bfloat16 [8, 2048, 4096], P('dp', 'ctx'), may hold values from -6 to 6
- attn_mix: bfloat16 [8, 2048, 4096], P('dp', 'ctx'), may hold values from -6 to 6
- mlp_in: bfloat16 [8, 2048, 4096], P('dp', 'ctx'), may hold values from -6 to 6
- mlp_act: bfloat16 [8, 2048, 14336], P('dp', 'ctx'), may hold values from -6 to 6
- grad_query: bfloat16 [8, 2048, 4096], P('dp', 'ctx'), may hold values from -0.19921875 to 0.19921875
- grad_key: bfloat16 [8, 2048, 1024], P('dp', 'ctx'), may hold values from -0.19921875 to 0.19921875
- grad_value: bfloat16 [8, 2048, 1024], P('dp', 'ctx'), may hold values from -0.19921875 to 0.19921875
- grad_output: bfloat16 [8, 2048, 4096], P('dp', 'ctx'), may hold values from -0.19921875 to 0.19921875
- grad_gate: bfloat16 [8, 2048, 14336], P('dp', 'ctx'), may hold values from -0.19921875 to 0.19921875
- grad_up: bfloat16 [8, 2048, 14336], P('dp', 'ctx'), may hold values from -0.19921875 to 0.19921875
- grad_down: bfloat16 [8, 2048, 4096], P('dp', 'ctx'), may hold values from -0.19921875 to 0.19921875
- proj_attn: bfloat16 [4096, 64], replicated, may hold values from -0.09375 to 0.09375
- proj_mix: bfloat16 [4096, 64], replicated, may hold values from -0.09375 to 0.09375
- proj_mlp: bfloat16 [4096, 64], replicated, may hold values from -0.09375 to 0.09375
- proj_act: bfloat16 [14336, 64], replicated, may hold values from -0.046875 to 0.046875
- proj_query: bfloat16 [4096, 64], replicated, may hold values from -0.09375 to 0.09375
- proj_key: bfloat16 [1024, 64], replicated, may hold values from -0.1875 to 0.1875
- proj_value: bfloat16 [1024, 64], replicated, may hold values from -0.1875 to 0.1875
- proj_output: bfloat16 [4096, 64], replicated, may hold values from -0.09375 to 0.09375
- proj_gate: bfloat16 [14336, 64], replicated, may hold values from -0.046875 to 0.046875
- proj_upward: bfloat16 [14336, 64], replicated, may hold values from -0.046875 to 0.046875
- proj_down: bfloat16 [4096, 64], replicated, may hold values from -0.09375 to 0.09375
- seq_counts: int32 [8], P('dp'), may hold values from 128 to 2048, as said below
- example_ids: int32 [8], replicated, may hold values from 0 to 7, each once
Outputs:
- store: float32 [8, 7, 4096], P('dp', None, 'ctx')
Inputs may be any that keep to these rules, and one draw needn't show every extreme that they name: `seq_counts`: every count is a multiple of 128; some sequence has all 2048 tokens. `example_ids`: a permutation: every store row receives exactly one sequence.
All inputs are finite; a program needn't handle non-finite values.
Results may differ from a plain program's by a relative error of at most 0.004.
Values sent between devices are 32-bit elements; how exact they have to be, the bound alone decides.
No kernel may reach another device: no remote copies, remote signals or barrier semaphores. Data moves between devices by JAX's collectives and lax.ppermute only.
A program may use at most 128 MiB of HBM per device.

v0:
```python
import jax
import jax.numpy as jnp
from jax import lax
from jax.sharding import PartitionSpec as P


def project_rows(acts, projection):
    return jnp.dot(acts[0], projection, preferred_element_type=jnp.float32).astype(jnp.bfloat16)


def outer_sum(grads_proj, inputs_proj):
    product = lax.dot_general(
        grads_proj, inputs_proj, (((0,), (0,)), ((), ())), preferred_element_type=jnp.float32
    )
    return product.reshape(-1)


def reduce_positions(values):
    summed = lax.psum(values, "ctx")
    width = values.shape[2] // lax.axis_size("ctx")
    return lax.dynamic_slice_in_dim(summed, lax.axis_index("ctx") * width, width, 2)


def pick_owned(gathered, example_ids):
    owner = lax.axis_index("dp")
    weights = (example_ids == owner).astype(jnp.float32)
    return jnp.sum(weights[:, None, None] * gathered, axis=0, keepdims=True)


def shards(
    attn_in,
    attn_mix,
    mlp_in,
    mlp_act,
    grad_query,
    grad_key,
    grad_value,
    grad_output,
    grad_gate,
    grad_up,
    grad_down,
    proj_attn,
    proj_mix,
    proj_mlp,
    proj_act,
    proj_query,
    proj_key,
    proj_value,
    proj_output,
    proj_gate,
    proj_upward,
    proj_down,
    seq_counts,
    example_ids,
):
    length_dev = attn_in.shape[1]
    first_pos = lax.axis_index("ctx") * length_dev
    limit_pos = seq_counts[0]
    live_rows = (first_pos + jnp.arange(length_dev, dtype=jnp.int32) < limit_pos).astype(
        jnp.bfloat16
    )[:, None]
    attn_p = project_rows(attn_in, proj_attn)
    mix_p = project_rows(attn_mix, proj_mix)
    mlp_p = project_rows(mlp_in, proj_mlp)
    act_p = project_rows(mlp_act, proj_act)
    pairs = [
        (grad_query, proj_query, attn_p),
        (grad_key, proj_key, attn_p),
        (grad_value, proj_value, attn_p),
        (grad_output, proj_output, mix_p),
        (grad_gate, proj_gate, mlp_p),
        (grad_up, proj_upward, mlp_p),
        (grad_down, proj_down, act_p),
    ]
    sketches = [
        outer_sum(project_rows(grads, projection) * live_rows, inputs_proj)
        for grads, projection, inputs_proj in pairs
    ]
    partial_sum = jnp.stack(sketches, axis=0)[None]
    shared = reduce_positions(partial_sum)
    gathered = lax.all_gather(shared, "dp", axis=0, tiled=True)
    return pick_owned(gathered, example_ids)


def solution(mesh):
    return jax.shard_map(
        shards,
        mesh=mesh,
        in_specs=(
            P("dp", "ctx", None),
            P("dp", "ctx", None),
            P("dp", "ctx", None),
            P("dp", "ctx", None),
            P("dp", "ctx", None),
            P("dp", "ctx", None),
            P("dp", "ctx", None),
            P("dp", "ctx", None),
            P("dp", "ctx", None),
            P("dp", "ctx", None),
            P("dp", "ctx", None),
            P(),
            P(),
            P(),
            P(),
            P(),
            P(),
            P(),
            P(),
            P(),
            P(),
            P(),
            P("dp"),
            P(),
        ),
        out_specs=P("dp", None, "ctx"),
        check_vma=False,
    )
```

profile of v0, /device:TPU:1, one launch (start us, length us, event | category | flops | bytes accessed | tf_op | source)
XLA Modules:
  0.0 140.8 jit_solution(12949452242620769150)
XLA Ops:
  7.3 1.8 %convolution_convert_fusion.6 = bf16[128,64]{0,1:T(8,128)(2,1)S(1)} fusion(bf16[4096,64]{0,1:T(8,128)(2,1)} %param.37, bf16[1,128,4096]{2,1,0:T(8,128)(2,1)} %param.26), kind=kOutput, calls=%fused_computation.29 | convolution fusion | flops 67117056 | bytes 1589248 | tf_op jit(solution)/shard_map/dot_general | solution.py:8
  9.2 3.3 %fusion.22 = f32[64,64]{1,0:T(8,128)S(1)} fusion(bf16[128,64]{0,1:T(8,128)(2,1)S(1)} %convolution_convert_fusion.6, bf16[14336,64]{0,1:T(8,128)(2,1)S(1)} %copy-done, bf16[1,128,14336]{2,1,0:T(8,128)(2,1)} %param.33, bf16[128]{0:T(256)(128)(2,1)S(1)} %compare_convert_fusion), kind=kOutput, calls=%fused_computation.17 | convolution fusion | flops 235945984 | bytes 5538048 | tf_op jit(solution)/shard_map/dot_general | solution.py:12
  12.5 0.1 stack_reshape.26
  12.6 4.0 %fusion.28 = f32[64,64]{1,0:T(8,128)S(1)} fusion(bf16[128,64]{0,1:T(8,128)(2,1)S(1)} %convolution_convert_fusion.6, bf16[14336,64]{0,1:T(8,128)(2,1)} %param.43, bf16[1,128,14336]{2,1,0:T(8,128)(2,1)} %param.32, bf16[128]{0:T(256)(128)(2,1)S(1)} %compare_convert_fusion), kind=kOutput, calls=%fused_computation.19 | convolution fusion | flops 235945984 | bytes 5538048 | tf_op jit(solution)/shard_map/dot_general | solution.py:12
  16.6 0.1 stack_reshape.25
  16.7 1.7 %convolution_convert_fusion.7 = bf16[128,64]{0,1:T(8,128)(2,1)S(1)} fusion(bf16[4096,64]{0,1:T(8,128)(2,1)S(1)} %copy-done.2, bf16[1,128,4096]{2,1,0:T(8,128)(2,1)} %param.24), kind=kOutput, calls=%fused_computation.30 | convolution fusion | flops 67117056 | bytes 1589248 | tf_op jit(solution)/shard_map/dot_general | solution.py:8
  18.4 1.4 %fusion.38 = f32[64,64]{1,0:T(8,128)S(1)} fusion(bf16[128,64]{0,1:T(8,128)(2,1)S(1)} %convolution_convert_fusion.7, bf16[1024,64]{0,1:T(8,128)(2,1)} %param.41, bf16[1,128,1024]{2,1,0:T(8,128)(2,1)} %param.30, bf16[128]{0:T(256)(128)(2,1)S(1)} %compare_convert_fusion), kind=kOutput, calls=%fused_computation.28 | convolution fusion | flops 17842176 | bytes 426240 | tf_op jit(solution)/shard_map/dot_general | solution.py:12
  19.8 0.1 stack_reshape.23
  20.0 1.4 fusion.36
  21.3 0.1 stack_reshape.22
  21.4 1.6 %fusion.31 = f32[64,64]{1,0:T(8,128)S(1)} fusion(bf16[128,64]{0,1:T(8,128)(2,1)S(1)} %convolution_convert_fusion.7, bf16[4096,64]{0,1:T(8,128)(2,1)} %param.39, bf16[1,128,4096]{2,1,0:T(8,128)(2,1)S(1)} %copy-done.1, bf16[128]{0:T(256)(128)(2,1)S(1)} %compare_convert_fusion), kind=kOutput, calls=%fused_computation.21 | convolution fusion | flops 68173824 | bytes 1605888 | tf_op jit(solution)/shard_map/dot_general | solution.py:12
  23.1 0.1 stack_reshape.21
  23.2 1.8 %convolution_convert_fusion.1 = bf16[128,64]{1,0:T(8,128)(2,1)S(1)} fusion(bf16[4096,64]{0,1:T(8,128)(2,1)} %param.36, bf16[1,128,4096]{2,1,0:T(8,128)(2,1)} %param.25), kind=kOutput, calls=%fused_computation.10 | convolution fusion | flops 67117056 | bytes 1589248 | tf_op jit(solution)/shard_map/dot_general | solution.py:8
  25.0 1.8 %fusion.33 = f32[64,64]{1,0:T(8,128)S(1)} fusion(bf16[128,64]{1,0:T(8,128)(2,1)S(1)} %convolution_convert_fusion.1, bf16[4096,64]{0,1:T(8,128)(2,1)S(1)} %copy-done.3, bf16[1,128,4096]{2,1,0:T(8,128)(2,1)} %param.31, bf16[128]{0:T(256)(128)(2,1)S(1)} %compare_convert_fusion), kind=kOutput, calls=%fused_computation.23 | convolution fusion | flops 68173824 | bytes 1605888 | tf_op jit(solution)/shard_map/dot_general | solution.py:12
  26.8 0.1 stack_reshape.24
  26.9 1.8 %fusion.34 = bf16[128,64]{1,0:T(8,128)(2,1)S(1)} fusion(bf16[4096,64]{0,1:T(8,128)(2,1)} %param.45, bf16[1,128,4096]{2,1,0:T(8,128)(2,1)} %param.34, bf16[128]{0:T(256)(128)(2,1)S(1)} %compare_convert_fusion), kind=kOutput, calls=%fused_computation.24 | convolution fusion | flops 67125248 | bytes 1589504 | tf_op jit(solution)/shard_map/dot_general | solution.py:8
  28.7 3.8 %fusion.16 = f32[64,64]{1,0:T(8,128)S(1)} fusion(bf16[128,64]{1,0:T(8,128)(2,1)S(1)} %fusion.34, bf16[14336,64]{0,1:T(8,128)(2,1)} %param.38, bf16[1,128,14336]{2,1,0:T(8,128)(2,1)} %param.27), kind=kOutput, calls=%fused_computation.15 | convolution fusion | flops 235937792 | bytes 5537792 | tf_op jit(solution)/shard_map/dot_general | solution.py:12
  32.5 0.1 stack_reshape.27
  32.6 0.8 stack.3
  33.5 83.8 %all-reduce.2.cloned.1.call-done = f32[1,7,4096]{2,1,0:T(8,128)} async-done(((f32[1,7,4096]{2,1,0:T(8,128)}), f32[1,7,4096]{2,1,0:T(8,128)}) %all-reduce.2.cloned.1.call-update) | async-done | bytes 114704 | tf_op jit(solution)/shard_map/psum | solution.py:19
  117.3 0.7 constant_dynamic-slice_fusion
  118.0 15.2 %all_gather.3 = f32[8,7,256]{2,1,0:T(8,128)S(1)} all-gather(f32[1,7,256]{2,1,0:T(8,128)S(1)} %constant_dynamic-slice_fusion), channel_id=1, replica_groups=mesh['dp'=8,'ctx'=16] {'dp'}, dimensions={0}, use_global_device_ids=true | all-gather | bytes 64512 | tf_op jit(solution)/shard_map/all_gather | solution.py:81
  133.3 0.1 multiply_reduce_fusion
  133.3 0.6 broadcast_in_dim.9
  (14 shorter events, 0.1 us)
Async XLA Ops:
  6.5 2.7 %copy-start = (bf16[14336,64]{0,1:T(8,128)(2,1)S(1)}, bf16[14336,64]{0,1:T(8,128)(2,1)}, u32[]{:S(2)}) copy-start(bf16[14336,64]{0,1:T(8,128)(2,1)} %param.44) | copy-start | bytes 5505028
  6.5 110.8 %all-reduce.2.cloned.1.call-start = ((), (), s32[]{:S(2)}) async-start(), calls=%async_computation | async-start | bytes 262144 | tf_op jit(solution)/shard_map/psum | solution.py:19
  12.5 4.2 %copy-start.2 = (bf16[4096,64]{0,1:T(8,128)(2,1)S(1)}, bf16[4096,64]{0,1:T(8,128)(2,1)}, u32[]{:S(2)}) copy-start(bf16[4096,64]{0,1:T(8,128)(2,1)} %param.35) | copy-start | bytes 1572868
  12.6 8.8 %copy-start.1 = (bf16[1,128,4096]{2,1,0:T(8,128)(2,1)S(1)}, bf16[1,128,4096]{2,1,0:T(8,128)(2,1)}, u32[]{:S(2)}) copy-start(bf16[1,128,4096]{2,1,0:T(8,128)(2,1)} %param.28) | copy-start | bytes 3145732
  18.4 6.6 %copy-start.3 = (bf16[4096,64]{0,1:T(8,128)(2,1)S(1)}, bf16[4096,64]{0,1:T(8,128)(2,1)}, u32[]{:S(2)}) copy-start(bf16[4096,64]{0,1:T(8,128)(2,1)} %param.42) | copy-start | bytes 1572868
  26.9 6.6 %copy-start.4 = (s32[8]{0:T(128)S(1)}, s32[8]{0:T(128)}, u32[]{:S(2)}) copy-start(s32[8]{0:T(128)} %param.47) | copy-start | bytes 100
Sparse Core Ops, SparseCore 0:
  33.6 83.6 all-reduce.1
where the time goes:
time: 141 us
  waiting for transfers between devices  83.8 us (59%)
  matrix products  24.4 us (17%)
  blocking collectives  15.2 us (11%)
  between operations  14.3 us (10%)
  local copies, waits for them, and re-layouts  2.84 us (2%)
    psum x1, waiting for transfers between devices, reduce_positions(): summed = lax.psum(values, 'ctx')  83.8 us
    dot_general x7, matrix products, outer_sum(): lax.dot_general(grads_proj, inputs_proj, (((0,), (0,)), ((), ())), prefer...  17.3 us
    all_gather x1, blocking collectives, shards(): gathered = lax.all_gather(shared, 'dp', axis=0, tiled=True)  15.2 us
    dot_general x4, matrix products, project_rows(): jnp.dot(acts[0], projection, preferred_element_type=jnp.float32)  7.1 us
  transfers between devices with their start and end apart: 1, of which 1 were waited for; matrix products, arithmetic and copies ran while one was open for 0% of the time, Pallas kernels for 0%

commit v1 on v0

--- a/solution.py
+++ b/solution.py
@@ -16,7 +16,9 @@
 
 
 def reduce_positions(values):
-    summed = lax.psum(values, "ctx")
+    summed = values
+    for hop in (1, 2, 4, 8):
+        summed = summed + lax.ppermute(summed, "ctx", [(dev, dev ^ hop) for dev in range(16)])
     width = values.shape[2] // lax.axis_size("ctx")
     return lax.dynamic_slice_in_dim(summed, lax.axis_index("ctx") * width, width, 2)
 

time: 141 us -> 66.5 us (0.47)
  waiting for transfers between devices: 83.8 us -> 10.9 us
  between operations: 14.3 us -> 0.96 us
  starting transfers between devices: 0.01 us -> 10.1 us
  blocking collectives: 15.2 us -> 17.6 us
    psum x1 -> x0, waiting for transfers between devices: 83.8 us -> none  [reduce_positions(): summed = lax.psum(values, 'ctx')]
    ppermute x0 -> x4, waiting for transfers between devices: none -> 10.9 us  [reduce_positions(): lax.ppermute(summed, 'ctx', [(dev, dev ^ hop) for dev in range(16)])]
    ppermute x0 -> x4, starting transfers between devices: none -> 10.1 us  [reduce_positions(): lax.ppermute(summed, 'ctx', [(dev, dev ^ hop) for dev in range(16)])]
    all_gather x1, blocking collectives: 15.2 us -> 17.6 us  [shards(): gathered = lax.all_gather(shared, 'dp', axis=0, tiled=True)]
  transfers between devices with their start and end apart: 1 -> 4, of which waited for: 1 -> 4; matrix products, arithmetic and copies ran while one was open for 0% -> 0% of each run, Pallas kernels for 0% -> 0%
where the time goes in v1:
time: 66.5 us; the launch traced here: 65.8 us
  matrix products  24.4 us (37%)
  blocking collectives  17.6 us (26%)
  waiting for transfers between devices  10.9 us (16%)
  starting transfers between devices  10.1 us (15%)
  local copies, waits for them, and re-layouts  1.51 us (2%)
  between operations  0.96 us (1%)
    all_gather x1, blocking collectives, shards(): gathered = lax.all_gather(shared, 'dp', axis=0, tiled=True)  17.6 us
    dot_general x7, matrix products, outer_sum(): lax.dot_general(grads_proj, inputs_proj, (((0,), (0,)), ((), ())), prefer...  17.3 us
    ppermute x4, waiting for transfers between devices, reduce_positions(): lax.ppermute(summed, 'ctx', [(dev, dev ^ hop) for dev in range(16)])  10.9 us
    ppermute x4, starting transfers between devices, reduce_positions(): lax.ppermute(summed, 'ctx', [(dev, dev ^ hop) for dev in range(16)])  10.1 us
    dot_general x4, matrix products, project_rows(): jnp.dot(acts[0], projection, preferred_element_type=jnp.float32)  7.1 us
  transfers between devices with their start and end apart: 4, of which 4 were waited for; matrix products, arithmetic and copies ran while one was open for 0% of the time, Pallas kernels for 0%

profile of v1, /device:TPU:1, one launch (start us, length us, event | category | flops | bytes accessed | tf_op | source)
XLA Modules:
  0.0 65.8 jit_solution(2322433838614786543)
XLA Ops:
  0.8 1.8 %convolution_convert_fusion.6 = bf16[128,64]{0,1:T(8,128)(2,1)S(1)} fusion(bf16[4096,64]{0,1:T(8,128)(2,1)} %param.37, bf16[1,128,4096]{2,1,0:T(8,128)(2,1)} %param.26), kind=kOutput, calls=%fused_computation.29 | convolution fusion | flops 67117056 | bytes 1589248 | tf_op jit(solution)/shard_map/dot_general | solution.py:8
  2.7 3.3 %fusion.22 = f32[64,64]{1,0:T(8,128)S(1)} fusion(bf16[128,64]{0,1:T(8,128)(2,1)S(1)} %convolution_convert_fusion.6, bf16[14336,64]{0,1:T(8,128)(2,1)S(1)} %copy-done, bf16[1,128,14336]{2,1,0:T(8,128)(2,1)} %param.33, bf16[128]{0:T(256)(128)(2,1)S(1)} %compare_convert_fusion), kind=kOutput, calls=%fused_computation.17 | convolution fusion | flops 235945984 | bytes 5538048 | tf_op jit(solution)/shard_map/dot_general | solution.py:12
  6.1 4.0 %fusion.28 = f32[64,64]{1,0:T(8,128)S(1)} fusion(bf16[128,64]{0,1:T(8,128)(2,1)S(1)} %convolution_convert_fusion.6, bf16[14336,64]{0,1:T(8,128)(2,1)} %param.43, bf16[1,128,14336]{2,1,0:T(8,128)(2,1)} %param.32, bf16[128]{0:T(256)(128)(2,1)S(1)} %compare_convert_fusion), kind=kOutput, calls=%fused_computation.19 | convolution fusion | flops 235945984 | bytes 5538048 | tf_op jit(solution)/shard_map/dot_general | solution.py:12
  10.2 1.7 %convolution_convert_fusion.7 = bf16[128,64]{0,1:T(8,128)(2,1)S(1)} fusion(bf16[4096,64]{0,1:T(8,128)(2,1)S(1)} %copy-done.2, bf16[1,128,4096]{2,1,0:T(8,128)(2,1)} %param.24), kind=kOutput, calls=%fused_computation.30 | convolution fusion | flops 67117056 | bytes 1589248 | tf_op jit(solution)/shard_map/dot_general | solution.py:8
  11.9 1.4 %fusion.38 = f32[64,64]{1,0:T(8,128)S(1)} fusion(bf16[128,64]{0,1:T(8,128)(2,1)S(1)} %convolution_convert_fusion.7, bf16[1024,64]{0,1:T(8,128)(2,1)} %param.41, bf16[1,128,1024]{2,1,0:T(8,128)(2,1)} %param.30, bf16[128]{0:T(256)(128)(2,1)S(1)} %compare_convert_fusion), kind=kOutput, calls=%fused_computation.28 | convolution fusion | flops 17842176 | bytes 426240 | tf_op jit(solution)/shard_map/dot_general | solution.py:12
  13.4 1.4 %fusion.36 = f32[64,64]{1,0:T(8,128)S(1)} fusion(bf16[128,64]{0,1:T(8,128)(2,1)S(1)} %convolution_convert_fusion.7, bf16[1024,64]{0,1:T(8,128)(2,1)} %param.40, bf16[1,128,1024]{2,1,0:T(8,128)(2,1)} %param.29, bf16[128]{0:T(256)(128)(2,1)S(1)} %compare_convert_fusion), kind=kOutput, calls=%fused_computation.26 | convolution fusion | flops 17842176 | bytes 426240 | tf_op jit(solution)/shard_map/dot_general | solution.py:12
  14.9 1.6 %fusion.31 = f32[64,64]{1,0:T(8,128)S(1)} fusion(bf16[128,64]{0,1:T(8,128)(2,1)S(1)} %convolution_convert_fusion.7, bf16[4096,64]{0,1:T(8,128)(2,1)} %param.39, bf16[1,128,4096]{2,1,0:T(8,128)(2,1)S(1)} %copy-done.1, bf16[128]{0:T(256)(128)(2,1)S(1)} %compare_convert_fusion), kind=kOutput, calls=%fused_computation.21 | convolution fusion | flops 68173824 | bytes 1605888 | tf_op jit(solution)/shard_map/dot_general | solution.py:12
  16.5 0.1 stack_reshape.21
  16.6 1.8 %convolution_convert_fusion.1 = bf16[128,64]{1,0:T(8,128)(2,1)S(1)} fusion(bf16[4096,64]{0,1:T(8,128)(2,1)} %param.36, bf16[1,128,4096]{2,1,0:T(8,128)(2,1)} %param.25), kind=kOutput, calls=%fused_computation.10 | convolution fusion | flops 67117056 | bytes 1589248 | tf_op jit(solution)/shard_map/dot_general | solution.py:8
  18.4 1.8 %fusion.33 = f32[64,64]{1,0:T(8,128)S(1)} fusion(bf16[128,64]{1,0:T(8,128)(2,1)S(1)} %convolution_convert_fusion.1, bf16[4096,64]{0,1:T(8,128)(2,1)S(1)} %copy-done.3, bf16[1,128,4096]{2,1,0:T(8,128)(2,1)} %param.31, bf16[128]{0:T(256)(128)(2,1)S(1)} %compare_convert_fusion), kind=kOutput, calls=%fused_computation.23 | convolution fusion | flops 68173824 | bytes 1605888 | tf_op jit(solution)/shard_map/dot_general | solution.py:12
  20.2 0.1 stack_reshape.24
  20.4 1.8 %fusion.34 = bf16[128,64]{1,0:T(8,128)(2,1)S(1)} fusion(bf16[4096,64]{0,1:T(8,128)(2,1)} %param.45, bf16[1,128,4096]{2,1,0:T(8,128)(2,1)} %param.34, bf16[128]{0:T(256)(128)(2,1)S(1)} %compare_convert_fusion), kind=kOutput, calls=%fused_computation.24 | convolution fusion | flops 67125248 | bytes 1589504 | tf_op jit(solution)/shard_map/dot_general | solution.py:8
  22.2 3.8 %fusion.16 = f32[64,64]{1,0:T(8,128)S(1)} fusion(bf16[128,64]{1,0:T(8,128)(2,1)S(1)} %fusion.34, bf16[14336,64]{0,1:T(8,128)(2,1)} %param.38, bf16[1,128,14336]{2,1,0:T(8,128)(2,1)} %param.27), kind=kOutput, calls=%fused_computation.15 | convolution fusion | flops 235937792 | bytes 5537792 | tf_op jit(solution)/shard_map/dot_general | solution.py:12
  26.1 0.2 stack.3
  26.3 2.1 %collective-permute-start = (f32[1,7,4096]{2,1,0:T(8,128)S(1)}, f32[1,7,4096]{2,1,0:T(8,128)S(1)}, u32[]{:S(2)}, u32[]{:S(2)}) collective-permute-start(f32[1,7,4096]{2,1,0:T(8,128)S(1)} %bitcast.75), channel_id=1, source_target_pairs={{0,1},{1,0},{2,3},{3,2},{4,5},{5,4},{6,7},{7,6},{8,9},{9,8},{10,11... | collective-permute-start | bytes 344072 | tf_op jit(solution)/shard_map/ppermute | solution.py:21
  28.4 2.7 %collective-permute-done = f32[1,7,4096]{2,1,0:T(8,128)S(1)} collective-permute-done((f32[1,7,4096]{2,1,0:T(8,128)S(1)}, f32[1,7,4096]{2,1,0:T(8,128)S(1)}, u32[]{:S(2)}, u32[]{:S(2)}) %collective-permute-start) | collective-permute-done | bytes 114720 | tf_op jit(solution)/shard_map/ppermute | solution.py:21
  31.1 3.3 %collective-permute-start.1 = (f32[1,7,4096]{2,1,0:T(8,128)S(1)}, f32[1,7,4096]{2,1,0:T(8,128)S(1)}, u32[]{:S(2)}, u32[]{:S(2)}) collective-permute-start(f32[1,7,4096]{2,1,0:T(8,128)S(1)} %bitcast_add_fusion), channel_id=1, source_target_pairs={{0,2},{1,3},{2,0},{3,1},{4,6},{5,7},{6,4},{7,5},{8,10},{9,11},{10,... | collective-permute-start | bytes 344072 | tf_op jit(solution)/shard_map/ppermute | solution.py:21
  34.4 2.4 %collective-permute-done.1 = f32[1,7,4096]{2,1,0:T(8,128)S(1)} collective-permute-done((f32[1,7,4096]{2,1,0:T(8,128)S(1)}, f32[1,7,4096]{2,1,0:T(8,128)S(1)}, u32[]{:S(2)}, u32[]{:S(2)}) %collective-permute-start.1) | collective-permute-done | bytes 114720 | tf_op jit(solution)/shard_map/ppermute | solution.py:21
  36.8 1.6 %collective-permute-start.2 = (f32[1,7,4096]{2,1,0:T(8,128)S(1)}, f32[1,7,4096]{2,1,0:T(8,128)S(1)}, u32[]{:S(2)}, u32[]{:S(2)}) collective-permute-start(f32[1,7,4096]{2,1,0:T(8,128)S(1)} %add.28), channel_id=1, source_target_pairs={{0,4},{1,5},{2,6},{3,7},{4,0},{5,1},{6,2},{7,3},{8,12},{9,13},{10,... | collective-permute-start | bytes 344072 | tf_op jit(solution)/shard_map/ppermute | solution.py:21
  38.4 2.4 %collective-permute-done.2 = f32[1,7,4096]{2,1,0:T(8,128)S(1)} collective-permute-done((f32[1,7,4096]{2,1,0:T(8,128)S(1)}, f32[1,7,4096]{2,1,0:T(8,128)S(1)}, u32[]{:S(2)}, u32[]{:S(2)}) %collective-permute-start.2) | collective-permute-done | bytes 114720 | tf_op jit(solution)/shard_map/ppermute | solution.py:21
  40.7 3.2 %collective-permute-start.3 = (f32[1,7,4096]{2,1,0:T(8,128)S(1)}, f32[1,7,4096]{2,1,0:T(8,128)S(1)}, u32[]{:S(2)}, u32[]{:S(2)}) collective-permute-start(f32[1,7,4096]{2,1,0:T(8,128)S(1)} %add.29), channel_id=1, source_target_pairs={{0,8},{1,9},{2,10},{3,11},{4,12},{5,13},{6,14},{7,15},{8,0},{9,1},... | collective-permute-start | bytes 344072 | tf_op jit(solution)/shard_map/ppermute | solution.py:21
  43.9 3.5 %collective-permute-done.3 = f32[1,7,4096]{2,1,0:T(8,128)S(1)} collective-permute-done((f32[1,7,4096]{2,1,0:T(8,128)S(1)}, f32[1,7,4096]{2,1,0:T(8,128)S(1)}, u32[]{:S(2)}, u32[]{:S(2)}) %collective-permute-start.3) | collective-permute-done | bytes 114720 | tf_op jit(solution)/shard_map/ppermute | solution.py:21
  47.4 17.6 %all_gather.3 = f32[8,7,256]{2,1,0:T(8,128)S(1)} all-gather(f32[1,7,256]{2,1,0:T(8,128)S(1)} %dynamic-slice_add_fusion), channel_id=1, replica_groups=mesh['dp'=8,'ctx'=16] {'dp'}, dimensions={0}, use_global_device_ids=true | all-gather | bytes 64512 | tf_op jit(solution)/shard_map/all_gather | solution.py:83
  65.1 0.6 broadcast_in_dim.9
  (22 shorter events, 0.7 us)
Async XLA Ops:
  0.0 2.6 %copy-start = (bf16[14336,64]{0,1:T(8,128)(2,1)S(1)}, bf16[14336,64]{0,1:T(8,128)(2,1)}, u32[]{:S(2)}) copy-start(bf16[14336,64]{0,1:T(8,128)(2,1)} %param.44) | copy-start | bytes 5505028
  6.0 4.2 %copy-start.2 = (bf16[4096,64]{0,1:T(8,128)(2,1)S(1)}, bf16[4096,64]{0,1:T(8,128)(2,1)}, u32[]{:S(2)}) copy-start(bf16[4096,64]{0,1:T(8,128)(2,1)} %param.35) | copy-start | bytes 1572868
  6.1 8.8 %copy-start.1 = (bf16[1,128,4096]{2,1,0:T(8,128)(2,1)S(1)}, bf16[1,128,4096]{2,1,0:T(8,128)(2,1)}, u32[]{:S(2)}) copy-start(bf16[1,128,4096]{2,1,0:T(8,128)(2,1)} %param.28) | copy-start | bytes 3145732
  11.9 6.6 %copy-start.3 = (bf16[4096,64]{0,1:T(8,128)(2,1)S(1)}, bf16[4096,64]{0,1:T(8,128)(2,1)}, u32[]{:S(2)}) copy-start(bf16[4096,64]{0,1:T(8,128)(2,1)} %param.42) | copy-start | bytes 1572868
  22.1 21.8 %copy-start.4 = (s32[8]{0:T(128)S(1)}, s32[8]{0:T(128)}, u32[]{:S(2)}) copy-start(s32[8]{0:T(128)} %param.47) | copy-start | bytes 100
  26.3 4.8 %collective-permute-start = (f32[1,7,4096]{2,1,0:T(8,128)S(1)}, f32[1,7,4096]{2,1,0:T(8,128)S(1)}, u32[]{:S(2)}, u32[]{:S(2)}) collective-permute-start(f32[1,7,4096]{2,1,0:T(8,128)S(1)} %bitcast.75), channel_id=1, source_target_pairs={{0,1},{1,0},{2,3},{3,2},{4,5},{5,4},{6,7},{7,6},{8,9},{9,8},{10,11... | collective-permute-start | bytes 344072 | tf_op jit(solution)/shard_map/ppermute | solution.py:21
  31.1 5.6 %collective-permute-start.1 = (f32[1,7,4096]{2,1,0:T(8,128)S(1)}, f32[1,7,4096]{2,1,0:T(8,128)S(1)}, u32[]{:S(2)}, u32[]{:S(2)}) collective-permute-start(f32[1,7,4096]{2,1,0:T(8,128)S(1)} %bitcast_add_fusion), channel_id=1, source_target_pairs={{0,2},{1,3},{2,0},{3,1},{4,6},{5,7},{6,4},{7,5},{8,10},{9,11},{10,... | collective-permute-start | bytes 344072 | tf_op jit(solution)/shard_map/ppermute | solution.py:21
  36.8 3.9 %collective-permute-start.2 = (f32[1,7,4096]{2,1,0:T(8,128)S(1)}, f32[1,7,4096]{2,1,0:T(8,128)S(1)}, u32[]{:S(2)}, u32[]{:S(2)}) collective-permute-start(f32[1,7,4096]{2,1,0:T(8,128)S(1)} %add.28), channel_id=1, source_target_pairs={{0,4},{1,5},{2,6},{3,7},{4,0},{5,1},{6,2},{7,3},{8,12},{9,13},{10,... | collective-permute-start | bytes 344072 | tf_op jit(solution)/shard_map/ppermute | solution.py:21
  40.7 6.7 %collective-permute-start.3 = (f32[1,7,4096]{2,1,0:T(8,128)S(1)}, f32[1,7,4096]{2,1,0:T(8,128)S(1)}, u32[]{:S(2)}, u32[]{:S(2)}) collective-permute-start(f32[1,7,4096]{2,1,0:T(8,128)S(1)} %add.29), channel_id=1, source_target_pairs={{0,8},{1,9},{2,10},{3,11},{4,12},{5,13},{6,14},{7,15},{8,0},{9,1},... | collective-permute-start | bytes 344072 | tf_op jit(solution)/shard_map/ppermute | solution.py:21
